TPU v7x, 128 devices: a whole 4x4x4 slice. The times are simulated.
128 devices in a mesh: gx: 8 (over y, core), yz: 16 (over z, x).
Axes of the slice: x: 4, y: 4, z: 4, core: 2. Of those that a mesh axis runs over, the one named last changes fastest.
Arguments:
- tokens: bfloat16 [768, 12288], P(None, ('gx', 'yz')), may hold values from -6 to 6
- gate_weight: bfloat16 [12288, 36864], P('gx', 'yz'), may hold values from -0.078125 to 0.078125
- up_weight: bfloat16 [12288, 36864], P('gx', 'yz'), may hold values from -0.078125 to 0.078125
- down_weight: bfloat16 [36864, 12288], P('yz', 'gx'), may hold values from -0.046875 to 0.046875
Outputs:
- mixed: bfloat16 [768, 12288], P(None, ('gx', 'yz'))
All inputs are finite; a program needn't handle non-finite values.
Results may differ from a plain program's by a relative error of at most 0.03.
Values may be sent and summed in bfloat16 or wider, within the bound.
A program may use at most 128 MiB of HBM per device.

v0:
```python
import jax
import jax.numpy as jnp
from jax import lax
from jax.sharding import PartitionSpec as P


def body(tokens, gate_weight, up_weight, down_weight):
    piece = lax.all_gather(tokens, "yz", axis=1, tiled=True)
    gate_part = jnp.dot(piece, gate_weight, preferred_element_type=jnp.float32)
    up_part = jnp.dot(piece, up_weight, preferred_element_type=jnp.float32)
    gate, up = (
        lax.psum_scatter(
            gate_part.astype(jnp.bfloat16), "gx", scatter_dimension=0, tiled=True
        ).astype(jnp.float32),
        lax.psum_scatter(
            up_part.astype(jnp.bfloat16), "gx", scatter_dimension=0, tiled=True
        ).astype(jnp.float32),
    )
    hidden_share = (jax.nn.silu(gate) * up).astype(jnp.bfloat16)
    terms = jnp.dot(
        lax.all_gather(hidden_share, "gx", axis=0, tiled=True),
        down_weight,
        preferred_element_type=jnp.float32,
    )
    return lax.psum_scatter(terms.astype(jnp.bfloat16), "yz", scatter_dimension=1, tiled=True)


def solution(mesh):
    placed = (P(None, ("gx", "yz")), P("gx", "yz"), P("gx", "yz"), P("yz", "gx"))
    return jax.shard_map(
        body, mesh=mesh, in_specs=placed, out_specs=P(None, ("gx", "yz")), check_vma=False
    )
```

profile of v0, /device:TPU:0, one launch (start us, length us, event | category | flops | bytes accessed | tf_op | source)
XLA Modules:
  0.0 264.8 jit_solution(13721223662786076555)
XLA Ops:
  6.5 0.0 all-gather.3.cloned.1.call-start
  6.5 0.7 all-gather.3.cloned.1.call-update
  7.3 0.0 reduce-scatter.6.cloned.1.call-start
  7.3 50.5 %all-gather.3.cloned.1.call-done = bf16[768,1536]{0,1:T(8,128)(2,1)} async-done(((bf16[768,96]{0,1:T(8,128)(2,1)}), bf16[768,1536]{0,1:T(8,128)(2,1)}) %all-gather.3.cloned.1.call-update) | async-done | bytes 2359312 | tf_op jit(solution)/shard_map/all_gather | solution.py:8
  57.8 10.5 %convolution_convert_fusion = bf16[768,2304]{1,0:T(8,128)(2,1)} fusion(bf16[768,1536]{0,1:T(8,128)(2,1)} %all-gather.3.cloned.1.call-done, bf16[1536,2304]{1,0:T(8,128)(2,1)} %param.6), kind=kOutput, calls=%fused_computation | convolution fusion | flops 5437587456 | bytes 12976128 | tf_op jit(solution)/shard_map/dot_general | solution.py:10
  68.3 0.0 copy-start
  68.3 0.0 reduce-scatter.6.cloned.1.call-update
  68.3 0.0 reduce-scatter.4.cloned.1.call-start
  68.4 1.6 copy-done
  70.0 10.2 %convolution_convert_fusion.1 = bf16[768,2304]{1,0:T(8,128)(2,1)} fusion(bf16[768,1536]{0,1:T(8,128)(2,1)S(1)} %copy-done, bf16[1536,2304]{1,0:T(8,128)(2,1)} %param.5), kind=kOutput, calls=%fused_computation.1 | convolution fusion | flops 5437587456 | bytes 12976128 | tf_op jit(solution)/shard_map/dot_general | solution.py:9
  80.2 0.0 reduce-scatter.4.cloned.1.call-update
  80.2 0.0 all-gather.5.cloned.1.call-start
  80.3 24.1 %reduce-scatter.6.cloned.1.call-done = bf16[96,2304]{1,0:T(8,128)(2,1)} async-done(((bf16[768,2304]{1,0:T(8,128)(2,1)}), bf16[96,2304]{1,0:T(8,128)(2,1)}) %reduce-scatter.6.cloned.1.call-update) | async-done | bytes 442384 | tf_op jit(solution)/shard_map/reduce_scatter | solution.py:15
  104.4 38.0 %reduce-scatter.4.cloned.1.call-done = bf16[96,2304]{1,0:T(8,128)(2,1)} async-done(((bf16[768,2304]{1,0:T(8,128)(2,1)}), bf16[96,2304]{1,0:T(8,128)(2,1)}) %reduce-scatter.4.cloned.1.call-update) | async-done | bytes 442384 | tf_op jit(solution)/shard_map/reduce_scatter | solution.py:12
  142.4 2.2 fusion.4
  144.6 0.0 all-gather.5.cloned.1.call-update
  144.6 0.0 reduce-scatter.8.cloned.1.call-start
  144.7 28.3 %all-gather.5.cloned.1.call-done = bf16[768,2304]{1,0:T(8,128)(2,1)} async-done(((bf16[96,2304]{1,0:T(8,128)(2,1)}), bf16[768,2304]{1,0:T(8,128)(2,1)}) %all-gather.5.cloned.1.call-update) | async-done | bytes 3538960 | tf_op jit(solution)/shard_map/all_gather | solution.py:21
  173.0 10.1 %convolution_convert_fusion.2 = bf16[768,1536]{0,1:T(8,128)(2,1)} fusion(bf16[768,2304]{1,0:T(8,128)(2,1)} %all-gather.5.cloned.1.call-done, bf16[2304,1536]{1,0:T(8,128)(2,1)} %param.7), kind=kOutput, calls=%fused_computation.2 | convolution fusion | flops 5436997632 | bytes 12976128 | tf_op jit(solution)/shard_map/dot_general | solution.py:20
  183.1 0.0 reduce-scatter.8.cloned.1.call-update
  183.1 75.2 %reduce-scatter.8.cloned.1.call-done = bf16[768,96]{0,1:T(8,128)(2,1)} async-done(((bf16[768,1536]{0,1:T(8,128)(2,1)}), bf16[768,96]{0,1:T(8,128)(2,1)}) %reduce-scatter.8.cloned.1.call-update) | async-done | bytes 147472 | tf_op jit(solution)/shard_map/reduce_scatter | solution.py:25
Async XLA Ops:
  6.5 51.3 %all-gather.3.cloned.1.call-start = ((), (), s32[]{:S(2)}) async-start(), calls=%async_computation.3 | async-start | bytes 2506752 | tf_op jit(solution)/shard_map/all_gather | solution.py:8
  7.3 97.1 %reduce-scatter.6.cloned.1.call-start = ((), (), s32[]{:S(2)}) async-start(), calls=%async_computation.5 | async-start | bytes 3981312 | tf_op jit(solution)/shard_map/reduce_scatter | solution.py:15
  68.3 1.7 copy-start
  68.3 74.1 %reduce-scatter.4.cloned.1.call-start = ((), (), s32[]{:S(2)}) async-start(), calls=%async_computation.4 | async-start | bytes 3981312 | tf_op jit(solution)/shard_map/reduce_scatter | solution.py:12
  80.2 92.8 %all-gather.5.cloned.1.call-start = ((), (), s32[]{:S(2)}) async-start(), calls=%async_computation.6 | async-start | bytes 3981312 | tf_op jit(solution)/shard_map/all_gather | solution.py:21
  144.6 113.7 %reduce-scatter.8.cloned.1.call-start = ((), (), s32[]{:S(2)}) async-start(), calls=%async_computation.7 | async-start | bytes 2506752 | tf_op jit(solution)/shard_map/reduce_scatter | solution.py:25
Sparse Core Ops, SparseCore 0:
  9.5 48.2 all-gather.2
  68.5 35.8 reduce-scatter.5
  106.9 35.4 reduce-scatter.3
  144.7 28.2 all-gather.4
  183.2 75.0 reduce-scatter.7
where the time goes:
time: 265 us
  waiting for transfers between devices  217 us (82%)
  matrix products  30.8 us (12%)
  between operations  13.1 us (5%)
    reduce_scatter x1, waiting for transfers between devices, body(): lax.psum_scatter(terms.astype(jnp.bfloat16), 'yz', scatter_dimension=1, t...  75.2 us
    all_gather x1, waiting for transfers between devices, body(): piece = lax.all_gather(tokens, 'yz', axis=1, tiled=True)  50.5 us
    reduce_scatter x1, waiting for transfers between devices, body(): lax.psum_scatter(gate_part.astype(jnp.bfloat16), 'gx', scatter_dimension=...  38 us
    all_gather x1, waiting for transfers between devices, body(): lax.all_gather(hidden_share, 'gx', axis=0, tiled=True)  28.3 us
    reduce_scatter x1, waiting for transfers between devices, body(): lax.psum_scatter(up_part.astype(jnp.bfloat16), 'gx', scatter_dimension=0,...  24.1 us
    dot_general x1, matrix products, body(): up_part = jnp.dot(piece, up_weight, preferred_element_type=jnp.float32)  10.5 us
    dot_general x1, matrix products, body(): gate_part = jnp.dot(piece, gate_weight, preferred_element_type=jnp.float32)  10.2 us
    dot_general x1, matrix products, body(): jnp.dot(lax.all_gather(hidden_share, 'gx', axis=0, tiled=True), down_weig...  10.1 us
  transfers between devices with their start and end apart: 5, of which 5 were waited for; matrix products, arithmetic and copies ran while one was open for 4% of the time, Pallas kernels for 0%

commit v1 on v0

v1 whole, which is shorter than its diff:
```python
import functools

import jax
import jax.numpy as jnp
from jax import lax
from jax.experimental import pallas as pl
from jax.experimental.pallas import tpu as pltpu
from jax.sharding import PartitionSpec as P

BF = jnp.bfloat16
F32 = jnp.float32
MESH = pl.DeviceIdType.MESH

ROWS = 768
R = 192
NI = ROWS // R
NJ = 3
S = NI * NJ
Q = R // 4
H = R // 2
K = 1536
FF = 2304
FH = FF // 2
FB = FH // NJ
ZB = 384
XB = 96


def kernel(tok_hbm, wg_hbm, wu_hbm, wd_hbm, out,
           wgu, wd, tok, tokx, sibs, sibr, par, own, yr, hid, terms, zr, xs, xr,
           w_sem, wd_sem, tl_sem, tx_s, tx_r, tz_s, tz_r,
           d_s, d_r, y_s, y_r, h_s, h_r, f_s, f_r, z_s, z_r, x_s, x_r):
    g = lax.axis_index("gx")
    s_ = lax.axis_index("yz")
    y, c = g // 2, g % 2
    z, x = s_ // 4, s_ % 4

    def m4(v):
        return lax.rem(v, 4)

    def at_y(v):
        return (m4(v) * 2 + c, s_)

    def at_z(v):
        return (g, m4(v) * 4 + x)

    def at_x(v):
        return (g, z * 4 + m4(v))

    sib_dev = (y * 2 + 1 - c, s_)
    yp, ym = at_y(y + 1), at_y(y + 3)
    zp, zm = at_z(z + 1), at_z(z + 3)
    xp, xm, xo = at_x(x + 1), at_x(x + 3), at_x(x + 2)

    def rc(src, dst, ss, rs, dev):
        return pltpu.make_async_remote_copy(
            src_ref=src, dst_ref=dst, send_sem=ss, recv_sem=rs,
            device_id=dev, device_id_type=MESH)

    def rows(q, n):
        return pl.ds(pl.multiple_of(q * n, 16), n)

    def lanes(b, n):
        return pl.ds(pl.multiple_of(b * n, 128), n)

    def w_copies(b):
        cols = lanes(b, FB)
        return (pltpu.make_async_copy(wg_hbm.at[:, cols], wgu.at[b, :, pl.ds(0, FB)], w_sem.at[b, 0]),
                pltpu.make_async_copy(wu_hbm.at[:, cols], wgu.at[b, :, pl.ds(FB, FB)], w_sem.at[b, 1]))

    def b_sib(j):
        return (1 - c) * NJ + j

    def b_own(j):
        return c * NJ + j

    tok_local = pltpu.make_async_copy(tok_hbm, tokx.at[x], tl_sem)
    tok_local.start()

    barrier = pltpu.get_barrier_semaphore()
    partners = (sib_dev, yp, ym, zp, zm, xp, xm, xo)
    for dev in partners:
        pl.semaphore_signal(barrier, inc=1, device_id=dev, device_id_type=MESH)
    for j in range(NJ):
        for b in (b_sib(j), b_own(j)):
            for cp in w_copies(b):
                cp.start()
    wd_copy = pltpu.make_async_copy(wd_hbm, wd, wd_sem)
    wd_copy.start()
    pl.semaphore_wait(barrier, len(partners))

    def tx_copy(i, d, dev):
        rr = rows(i, R)
        return rc(tok_hbm.at[rr], tokx.at[x, rr], tx_s.at[i, d], tx_r.at[i, d], dev)

    for i in range(NI):
        for d, dev in enumerate((xp, xm, xo)):
            tx_copy(i, d, dev).start()

    def tz_copy(i, d):
        blk = tok.at[i, :, lanes(z, ZB)]
        return rc(blk, blk, tz_s.at[i, d], tz_r.at[i, d], zp if d == 0 else zm)

    def tz_recv(i, d):
        blk = tok.at[i, :, lanes(m4(z + 3) if d == 0 else m4(z + 1), ZB)]
        return rc(blk, blk, tz_s.at[i, d], tz_r.at[i, d], zp)

    def tf_copy(i, d):
        blk = tok.at[i, pl.ds(d * H, H), lanes(m4(z + 3) if d == 0 else m4(z + 1), ZB)]
        return rc(blk, blk, tz_s.at[i, 2 + d], tz_r.at[i, 2 + d], zp if d == 0 else zm)

    def tf_recv(i, d):
        blk = tok.at[i, pl.ds(d * H, H), lanes(m4(z + 2), ZB)]
        return rc(blk, blk, tz_s.at[i, 2 + d], tz_r.at[i, 2 + d], zp)

    def tok_spread(i):
        rr = rows(i, R)
        for d, dev in enumerate((xp, xm, xo)):
            tx_copy(i, d, dev).wait()
        tok[i, :, lanes(z, ZB)] = jnp.concatenate([tokx[k, rr, :] for k in range(4)], axis=1)
        for d in range(2):
            tz_copy(i, d).start()

    def tok_forward(i):
        for d in range(2):
            tz_recv(i, d).wait_recv()
            tf_copy(i, d).start()

    def tok_ready(i):
        for d in range(2):
            tf_recv(i, d).wait_recv()
            tz_copy(i, d).wait_send()
            tf_copy(i, d).wait_send()

    tok_local.wait()
    tok_spread(0)
    tok_forward(0)
    tok_spread(1)

    def d_copy(s):
        return rc(sibs.at[s], sibr.at[s], d_s.at[s], d_r.at[s], sib_dev)

    def stage_sib(s):
        i, j = s // NJ, s % NJ

        @pl.when(j == 0)
        def _():
            tok_ready(i)

        @pl.when(i == 0)
        def _():
            for cp in w_copies(b_sib(j)):
                cp.wait()

        sibs[s] = jnp.dot(tok[i], wgu[b_sib(j)], preferred_element_type=F32).astype(BF)
        d_copy(s).start()

    def stage_own(s):
        i, j = s // NJ, s % NJ

        @pl.when(i == 0)
        def _():
            for cp in w_copies(b_own(j)):
                cp.wait()

        own[...] = jnp.dot(tok[i], wgu[b_own(j)], preferred_element_type=F32)

    G, U = pl.ds(0, FB), pl.ds(FB, FB)

    def y_copy(s, n):
        if n == 0:
            src, dev = par.at[s, rows(m4(y + 2), Q), G], yp
        elif n == 1:
            src, dev = par.at[s, rows(m4(y + 2), Q), U], ym
        elif n == 2:
            src, dev = par.at[s, rows(m4(y + 1), Q), U], yp
        elif n == 3:
            src, dev = par.at[s, rows(m4(y + 3), Q), G], ym
        elif n == 4:
            src, dev = par.at[s, rows(m4(y + 1), Q), G], yp
        else:
            src, dev = par.at[s, rows(m4(y + 3), Q), U], ym
        return rc(src, yr.at[s, n], y_s.at[s, n], y_r.at[s, n], dev)

    def stage_merge(s):
        d_copy(s).wait()
        par[s] = (own[...] + sibr[s].astype(F32)).astype(BF)
        for n in range(4):
            y_copy(s, n).start()

    def stage_c(s):
        y_copy(s, 0).wait()
        rr = rows(m4(y + 1), Q)
        par[s, rr, G] = (par[s, rr, G].astype(F32) + yr[s, 0].astype(F32)).astype(BF)
        y_copy(s, 4).start()
        y_copy(s, 1).wait()
        rr = rows(m4(y + 3), Q)
        par[s, rr, U] = (par[s, rr, U].astype(F32) + yr[s, 1].astype(F32)).astype(BF)
        y_copy(s, 5).start()

    def h_block(s, yy):
        i, j = s // NJ, s % NJ
        return hid.at[i, rows(m4(yy), Q), lanes(b_own(j), FB)]

    def h_copy(s, d):
        blk = h_block(s, y)
        return rc(blk, blk, h_s.at[s, d], h_r.at[s, d], yp if d == 0 else ym)

    def h_recv(s, d):
        blk = h_block(s, y + 3 if d == 0 else y + 1)
        return rc(blk, blk, h_s.at[s, d], h_r.at[s, d], yp)

    def hf_copy(s, d):
        blk = h_block(s, y + 3 if d == 0 else y + 1)
        return rc(blk, blk, h_s.at[s, 2], h_r.at[s, 2], yp if d == 0 else ym)

    def hf_recv(s):
        blk = h_block(s, y + 2)
        return rc(blk, blk, h_s.at[s, 2], h_r.at[s, 2], yp)

    def stage_d(s):
        i, j = s // NJ, s % NJ
        for n in range(2, 6):
            y_copy(s, n).wait()
        rr = rows(y, Q)
        gate = par[s, rr, G].astype(F32) + (yr[s, 3].astype(F32) + yr[s, 4].astype(F32))
        up = par[s, rr, U].astype(F32) + (yr[s, 2].astype(F32) + yr[s, 5].astype(F32))
        hid[i, rr, lanes(b_own(j), FB)] = (gate / (1.0 + jnp.exp(-gate)) * up).astype(BF)
        for d in range(2):
            h_copy(s, d).start()

    def stage_e(s):
        for d in range(2):
            h_copy(s, d).wait_send()
            h_recv(s, d).wait_recv()

        @pl.when(s % 2 == 0)
        def _():
            hf_copy(s, 0).start()

        @pl.when(s % 2 == 1)
        def _():
            hf_copy(s, 1).start()

    def f_copy(s, half):
        i, j = s // NJ, s % NJ
        blk = hid.at[i, :, lanes(half * NJ + j, FB)]
        return rc(blk, blk, f_s.at[s], f_r.at[s], sib_dev)

    def stage_f(s):
        hf_recv(s).wait_recv()
        hf_copy(s, 0).wait_send()
        f_copy(s, c).start()

    def zb(k):
        return lanes(m4(z + k), ZB)

    A, B = pl.ds(0, H), pl.ds(H, H)

    def z_copy(i, n):
        half, k, dev = ((A, 2, zp), (B, 2, zm), (B, 1, zp), (A, 3, zm), (A, 1, zp), (B, 3, zm))[n]
        return rc(terms.at[i, half, zb(k)], zr.at[i, n], z_s.at[i, n], z_r.at[i, n], dev)

    def stage_g(i):
        @pl.when(i == 0)
        def _():
            wd_copy.wait()

        for j in range(NJ):
            f_copy(i * NJ + j, c).wait_send()
            f_copy(i * NJ + j, 1 - c).wait_recv()
        first = m4(z + 2) // 2
        for n in range(2):
            cols = lanes(first if n == 0 else 1 - first, 2 * ZB)
            terms[i, :, cols] = jnp.dot(hid[i], wd[:, cols], preferred_element_type=F32).astype(BF)
            if n == 0:
                z_copy(i, 0).start()
                z_copy(i, 1).start()
        z_copy(i, 2).start()
        z_copy(i, 3).start()

    def stage_z(i):
        z_copy(i, 0).wait()
        terms[i, A, zb(1)] = (terms[i, A, zb(1)].astype(F32) + zr[i, 0].astype(F32)).astype(BF)
        z_copy(i, 4).start()
        z_copy(i, 1).wait()
        terms[i, B, zb(3)] = (terms[i, B, zb(3)].astype(F32) + zr[i, 1].astype(F32)).astype(BF)
        z_copy(i, 5).start()

    def x_copy(i, d):
        k, dev = ((1, xp), (3, xm), (2, xo))[d]
        return rc(xs.at[i, m4(x + k)], xr.at[i, d], x_s.at[i, d], x_r.at[i, d], dev)

    def stage_x(i):
        for n in range(2, 6):
            z_copy(i, n).wait()
        for half, n1, n2 in ((A, 3, 4), (B, 2, 5)):
            v = terms[i, half, zb(0)].astype(F32) + (zr[i, n1].astype(F32) + zr[i, n2].astype(F32))
            for k in range(4):
                xs[i, k, half, :] = v[:, k * XB:(k + 1) * XB].astype(BF)
        for d in range(3):
            x_copy(i, d).start()

    def stage_out(i):
        for d in range(3):
            x_copy(i, d).wait()
        v = xs[i, x].astype(F32)
        for d in range(3):
            v = v + xr[i, d].astype(F32)
        out[rows(i, R), :] = v.astype(BF)

    def step(u, _):
        t = u - 1

        @pl.when((t >= 0) & (t < S))
        def _():
            stage_own(t)

        @pl.when(t + 1 < S)
        def _():
            stage_sib(t + 1)

        @pl.when((t >= 0) & (t < S))
        def _():
            stage_merge(t)

        def lag(n, f):
            s = t - n

            @pl.when((s >= 0) & (s < S))
            def _():
                f(s)

        def lag_i(n, f):
            s = t - n

            @pl.when((s >= 0) & (s < S) & (lax.rem(s + S, NJ) == NJ - 1))
            def _():
                f(s // NJ)

        lag(1, stage_c)
        lag(2, stage_d)
        lag(3, stage_e)
        lag(4, stage_f)

        i, j = t // NJ, t % NJ

        @pl.when((t >= 0) & (j == 0) & (i + 1 < NI))
        def _():
            tok_forward(i + 1)

            @pl.when(i + 2 < NI)
            def _():
                tok_spread(i + 2)

        lag_i(5, stage_g)
        lag_i(6, stage_z)
        lag_i(7, stage_x)
        lag_i(8, stage_out)
        return 0

    lax.fori_loop(0, S + 9, step, 0)


def body(tokens, gate_weight, up_weight, down_weight):
    V = pltpu.VMEM
    D = pltpu.SemaphoreType.DMA
    return pl.pallas_call(
        kernel,
        out_shape=jax.ShapeDtypeStruct((ROWS, XB), BF),
        in_specs=[pl.BlockSpec(memory_space=pl.ANY)] * 4,
        out_specs=pl.BlockSpec(memory_space=V),
        scratch_shapes=[
            V((2 * NJ, K, 2 * FB), BF),
            V((FF, K), BF),
            V((NI, R, K), BF),
            V((4, ROWS, XB), BF),
            V((S, R, 2 * FB), BF),
            V((S, R, 2 * FB), BF),
            V((S, R, 2 * FB), BF),
            V((R, 2 * FB), F32),
            V((S, 6, Q, FB), BF),
            V((NI, R, FF), BF),
            V((NI, R, K), BF),
            V((NI, 6, H, ZB), BF),
            V((NI, 4, R, XB), BF),
            V((NI, 3, R, XB), BF),
            D((2 * NJ, 2)), D(()), D(()),
            D((NI, 3)), D((NI, 3)), D((NI, 4)), D((NI, 4)),
            D((S,)), D((S,)), D((S, 6)), D((S, 6)), D((S, 3)), D((S, 3)), D((S,)), D((S,)),
            D((NI, 6)), D((NI, 6)), D((NI, 3)), D((NI, 3)),
        ],
        compiler_params=pltpu.CompilerParams(
            collective_id=0, has_side_effects=True, vmem_limit_bytes=60 * 2**20),
    )(tokens, gate_weight, up_weight, down_weight)


def solution(mesh):
    placed = (P(None, ("gx", "yz")), P("gx", "yz"), P("gx", "yz"), P("yz", "gx"))
    return jax.shard_map(
        body, mesh=mesh, in_specs=placed, out_specs=P(None, ("gx", "yz")), check_vma=False
    )
```

time: 265 us -> 107 us (0.40)
  waiting for transfers between devices: 217 us -> 0 us
  Pallas kernels: 0 us -> 103 us
  matrix products: 30.8 us -> 0 us
  between operations: 13.1 us -> 0.01 us
    reduce_scatter x3 -> x0, waiting for transfers between devices: 137 us -> none  [the longest x1 75.2 us: body(): lax.psum_scatter(terms.astype(jnp.bfloat16), 'yz', scatter_dimension=1, t...]
    pallas_call x0 -> x1, Pallas kernels: none -> 103 us  [body(): pl.pallas_call(kernel, out_shape=jax.ShapeDtypeStruct((ROWS, XB), BF), in...]
    all_gather x2 -> x0, waiting for transfers between devices: 78.8 us -> none  [the longest x1 50.5 us: body(): piece = lax.all_gather(tokens, 'yz', axis=1, tiled=True)]
    dot_general x3 -> x0, matrix products: 30.8 us -> none  [the longest x1 10.5 us: body(): up_part = jnp.dot(piece, up_weight, preferred_element_type=jnp.float32)]
  transfers between devices with their start and end apart: 5 -> 0, of which waited for: 5 -> 0; matrix products, arithmetic and copies ran while one was open for 4% -> 0% of each run, Pallas kernels for 0% -> 0%
where the time goes in v1:
time: 107 us
  Pallas kernels  103 us (96%)
  local copies, waits for them, and re-layouts  3.43 us (3%)
    pallas_call x1, Pallas kernels, body(): pl.pallas_call(kernel, out_shape=jax.ShapeDtypeStruct((ROWS, XB), BF), in...  103 us

profile of v1, /device:TPU:0, one launch (start us, length us, event | category | flops | bytes accessed | tf_op | source)
XLA Modules:
  0.0 106.8 jit_solution(18014596350115659132)
XLA Ops:
  0.0 1.7 %copy.5.tok_hbm = bf16[768,96]{1,0:T(8,128)(2,1)} copy(bf16[768,96]{0,1:T(8,128)(2,1)} %param.4) | data formatting | bytes 294912 | tf_op args[0]
  1.7 103.3 %shard_map.46 = bf16[768,96]{1,0:T(8,128)(2,1)} custom-call(bf16[768,96]{1,0:T(8,128)(2,1)} %copy.5.tok_hbm, bf16[1536,2304]{1,0:T(8,128)(2,1)} %wg_hbm.1, bf16[1536,2304]{1,0:T(8,128)(2,1)} %wu_hbm.1, bf16[2304,1536]{1,0:T(8,128)(2,1)} %wd_hbm.1), custom_call_target="tpu_custom_call" | custom-call | tf_op jit(solution)/shard_map/pallas_call | solution.py:368
  105.0 1.7 %copy.6 = bf16[768,96]{0,1:T(8,128)(2,1)} copy(bf16[768,96]{1,0:T(8,128)(2,1)} %shard_map.46) | data formatting | bytes 294912 | tf_op jit(solution)/shard_map/pallas_call | solution.py:368

commit v2 on v0

v2 whole, which is shorter than its diff:
```python
import jax
import jax.numpy as jnp
from jax import lax
from jax.experimental import pallas as pl
from jax.experimental.pallas import tpu as pltpu
from jax.sharding import PartitionSpec as P

BF = jnp.bfloat16
F32 = jnp.float32
MESH = pl.DeviceIdType.MESH

ROWS = 768
R = 128
NI = ROWS // R
NJ = 3
S = NI * NJ
Q = R // 4
K = 1536
FF = 2304
FB = FF // 2 // NJ
XB = 96
HB = XB // 2

LC, LD, LE, LF, LG, LZ, LO = 3, 5, 7, 9, 10, 12, 14
DIRECT = S - 1


def kernel(tok_hbm, wg_hbm, wu_hbm, wd_hbm, out,
           wgu, wd, tok, tokr, sibs, sibr, par, own, yr, hid, terms, r1, r2,
           w_sem, wd_sem, tl_sem, t1_s, t1_r, t2_s, t2_r,
           d_s, d_r, y_s, c_r, e_r, h_s, h_r, hf_r, f_s, f_r, z1_s, z1_r, z2_s, z2_r):
    g = lax.axis_index("gx")
    s_ = lax.axis_index("yz")
    y, c = g // 2, g % 2
    z, x = s_ // 4, s_ % 4

    def m4(v):
        return lax.rem(v, 4)

    sib_dev = (y * 2 + 1 - c, s_)
    yp, ym, yo = (m4(y + 1) * 2 + c, s_), (m4(y + 3) * 2 + c, s_), (m4(y + 2) * 2 + c, s_)

    def at_z(k):
        return (g, m4(z + k) * 4 + x)

    def at_x(k):
        return (g, z * 4 + m4(x + k))

    def rc(src, dst, ss, rs, dev):
        return pltpu.make_async_remote_copy(
            src_ref=src, dst_ref=dst, send_sem=ss, recv_sem=rs,
            device_id=dev, device_id_type=MESH)

    def arrived(ref, sem):
        rc(ref, ref, y_s, sem, sib_dev).wait_recv()

    def sent(ref, sem):
        rc(ref, ref, sem, d_r.at[0], sib_dev).wait_send()

    def rows(q, n):
        return pl.ds(pl.multiple_of(q * n, 16), n)

    def lanes(b, n):
        return pl.ds(pl.multiple_of(b * n, 128), n)

    A, B = pl.ds(0, HB), pl.ds(HB, HB)

    barrier = pltpu.get_barrier_semaphore()
    partners = [sib_dev, yp, ym, yo] + [f(k) for k in (1, 2, 3) for f in (at_z, at_x)]
    for dev in partners:
        pl.semaphore_signal(barrier, inc=1, device_id=dev, device_id_type=MESH)

    def b_sib(j):
        return (1 - c) * NJ + j

    def b_own(j):
        return c * NJ + j

    def tl_copy(i):
        return pltpu.make_async_copy(tok_hbm.at[:, pl.ds(i * R, R)], tok.at[i, z, x], tl_sem)

    for i in range(NI):
        tl_copy(i).start()

    def w_copies(b):
        cols = lanes(b, FB)
        return (pltpu.make_async_copy(wg_hbm.at[:, cols], wgu.at[b, :, pl.ds(0, FB)], w_sem.at[b]),
                pltpu.make_async_copy(wu_hbm.at[:, cols], wgu.at[b, :, pl.ds(FB, FB)], w_sem.at[b]))

    def w_arrived(b):
        pltpu.make_async_copy(wgu.at[b], wgu.at[b], w_sem.at[b]).wait()

    wd_copy = pltpu.make_async_copy(wd_hbm, wd, wd_sem)

    def weights_start():
        for j in range(NJ):
            for b in (b_sib(j), b_own(j)):
                for cp in w_copies(b):
                    cp.start()
        wd_copy.start()

    def t1_copy(i, h, k):
        cols = pl.ds(pl.multiple_of(i * R, R), R)
        half = A if h == 0 else B
        return rc(tok_hbm.at[half, cols], tok.at[i, z, x, half], t1_s, t1_r.at[i],
                  at_x(k) if h == 0 else at_z(k))

    def t2_copy(i, h, k):
        blk = tok.at[i, z, :, A] if h == 0 else tok.at[i, :, x, B]
        return rc(blk, blk, t2_s, t2_r.at[i], at_z(k) if h == 0 else at_x(k))

    BOTH = [(h, k) for k in (2, 1, 3) for h in (0, 1)]

    def tok_first(i):
        for h, k in BOTH:
            t1_copy(i, h, k).start()

    def tok_second(i):
        arrived(r2.at[i], t1_r.at[i])
        for h, k in BOTH:
            t2_copy(i, h, k).start()

    def tok_ready(i):
        arrived(r1.at[i], t2_r.at[i])
        tokr[i % 2] = tok[i].reshape(K, R).T

    def entry_barrier():
        pl.semaphore_wait(barrier, len(partners))

    def entry_own():
        pltpu.make_async_copy(tok.at[:, 0, 0], tok.at[:, 0, 0], tl_sem).wait()

    entry_barrier()
    tok_first(0)
    weights_start()
    entry_own()
    tok_second(0)
    tok_first(1)

    def d_copy(s):
        return rc(sibs.at[s], sibr.at[s], d_s, d_r.at[s], sib_dev)

    def stage_sib(s):
        i, j = s // NJ, s % NJ

        @pl.when(j == 0)
        def _():
            tok_ready(i)

        @pl.when(i == 0)
        def _():
            w_arrived(b_sib(j))

        sibs[s] = jnp.dot(tokr[i % 2], wgu[b_sib(j)], preferred_element_type=F32).astype(BF)
        d_copy(s).start()

        @pl.when((j == 0) & (i + 1 < NI))
        def _():
            tok_second(i + 1)

            @pl.when(i + 2 < NI)
            def _():
                tok_first(i + 2)

    def stage_own(s):
        i, j = s // NJ, s % NJ

        @pl.when(i == 0)
        def _():
            w_arrived(b_own(j))

        own[...] = jnp.dot(tokr[i % 2], wgu[b_own(j)], preferred_element_type=F32)

    G, U = pl.ds(0, FB), pl.ds(FB, FB)

    def y_copy(s, n):
        q, cols, dev = ((2, G, yp), (2, U, ym), (1, U, yp), (3, G, ym), (1, G, yp), (3, U, ym))[n]
        return rc(par.at[s, rows(m4(y + q), Q), cols], yr.at[s, n], y_s, (c_r if n < 2 else e_r).at[s], dev)

    def stage_merge(s):
        arrived(sibr.at[s], d_r.at[s])
        par[s] = (own[...] + sibr[s].astype(F32)).astype(BF)
        for n in range(4):
            y_copy(s, n).start()

    def stage_c(s):
        arrived(yr.at[s, pl.ds(0, 2)], c_r.at[s])
        rr = rows(m4(y + 1), Q)
        par[s, rr, G] = (par[s, rr, G].astype(F32) + yr[s, 0].astype(F32)).astype(BF)
        y_copy(s, 4).start()
        rr = rows(m4(y + 3), Q)
        par[s, rr, U] = (par[s, rr, U].astype(F32) + yr[s, 1].astype(F32)).astype(BF)
        y_copy(s, 5).start()

    def h_block(s, k):
        i, j = s // NJ, s % NJ
        return hid.at[i, rows(m4(y + k), Q), lanes(b_own(j), FB)]

    def h_copy(s, d):
        blk = h_block(s, 0)
        return rc(blk, blk, h_s, h_r.at[s], yp if d == 0 else ym)

    def hf_copy(s, d):
        blk = h_block(s, 3 if d == 0 else 1)
        return rc(blk, blk, h_s, hf_r.at[s], yp if d == 0 else ym)

    def ho_copy(s):
        blk = h_block(s, 0)
        return rc(blk, blk, h_s, hf_r.at[s], yo)

    def stage_d(s):
        i, j = s // NJ, s % NJ
        arrived(yr.at[s, pl.ds(2, 4)], e_r.at[s])
        rr = rows(y, Q)
        gate = par[s, rr, G].astype(F32) + (yr[s, 3].astype(F32) + yr[s, 4].astype(F32))
        up = par[s, rr, U].astype(F32) + (yr[s, 2].astype(F32) + yr[s, 5].astype(F32))
        hid[i, rr, lanes(b_own(j), FB)] = (gate / (1.0 + jnp.exp(-gate)) * up).astype(BF)
        @pl.when(s >= DIRECT)
        def _():
            ho_copy(s).start()

        for d in range(2):
            h_copy(s, d).start()

    def stage_e(s):
        arrived(yr.at[s, pl.ds(0, 2)], h_r.at[s])

        @pl.when((s < DIRECT) & (s % 2 == 0))
        def _():
            hf_copy(s, 0).start()

        @pl.when((s < DIRECT) & (s % 2 == 1))
        def _():
            hf_copy(s, 1).start()

    def f_copy(s, half):
        i, j = s // NJ, s % NJ
        blk = hid.at[i, :, lanes(half * NJ + j, FB)]
        return rc(blk, blk, f_s, f_r.at[i], sib_dev)

    def stage_f(s):
        arrived(yr.at[s, 0], hf_r.at[s])
        f_copy(s, c).start()

    def z1_copy(i, h, k):
        if h == 0:
            src, dev = terms.at[i, m4(z + k), :, A], at_z(k)
        else:
            src, dev = terms.at[i, :, m4(x + k), B], at_x(k)
        return rc(src, r1.at[i, h, k - 1], z1_s, z1_r.at[i], dev)

    def z2_copy(i, h, k):
        if h == 0:
            src, dev = terms.at[i, z, m4(x + k), A], at_x(k)
        else:
            src, dev = terms.at[i, m4(z + k), x, B], at_z(k)
        return rc(src, r2.at[i, h, k - 1], z2_s, z2_r.at[i], dev)

    def stage_g(i):
        @pl.when(i == 0)
        def _():
            wd_copy.wait()

        arrived(hid.at[i, :, pl.ds(0, FF // 2)], f_r.at[i])
        mine = z // 2
        for n in range(2):
            p = mine if n else 1 - mine
            res = jnp.dot(hid[i], wd[:, lanes(p, K // 2)], preferred_element_type=F32).astype(BF)
            terms[i, pl.ds(2 * p, 2)] = res.T.reshape(2, 4, XB, R)
        for h, k in BOTH:
            z1_copy(i, h, k).start()

    def stage_z(i):
        arrived(r1.at[i], z1_r.at[i])
        for h in (0, 1):
            v = r1[i, h, 0].astype(F32) + r1[i, h, 1].astype(F32) + r1[i, h, 2].astype(F32)
            if h == 0:
                terms[i, z, :, A] = (terms[i, z, :, A].astype(F32) + v).astype(BF)
            else:
                terms[i, :, x, B] = (terms[i, :, x, B].astype(F32) + v).astype(BF)
            for k in (2, 1, 3):
                z2_copy(i, h, k).start()

    def stage_out(i):
        cols = lanes(i, R)
        arrived(r2.at[i], z2_r.at[i])
        for h, half in ((0, A), (1, B)):
            v = terms[i, z, x, half].astype(F32)
            for k in (0, 1, 2):
                v = v + r2[i, h, k].astype(F32)
            out[half, cols] = v.astype(BF)

    def step(u, _):
        t = u - 1

        @pl.when((t >= 0) & (t < S))
        def _():
            stage_own(t)
            stage_merge(t)

        @pl.when(t + 1 < S)
        def _():
            stage_sib(t + 1)

        def lag(n, f):
            s = t - n

            @pl.when((s >= 0) & (s < S))
            def _():
                f(s)

        def lag_i(n, f, most):
            s = t - n

            @pl.when((s >= 0) & (s < most * NJ) & (lax.rem(s + S, NJ) == NJ - 1))
            def _():
                f(s // NJ)

        lag(LC, stage_c)
        lag(LD, stage_d)
        lag(LE, stage_e)
        lag(LF, stage_f)
        lag_i(LG, stage_g, NI - 1)
        lag_i(LZ, stage_z, NI - 2)
        lag_i(LO, stage_out, NI - 2)
        return 0

    lax.fori_loop(0, S + LF + 1, step, 0)
    stage_g(NI - 1)
    stage_z(NI - 2)
    stage_z(NI - 1)
    stage_out(NI - 2)
    stage_out(NI - 1)

    def entry_sent():
        for ref, sem in ((r2, t1_s), (r1, t2_s), (sibs, d_s), (yr, y_s), (yr.at[:, pl.ds(0, 3)], h_s),
                         (hid.at[:, :, pl.ds(0, FF // 2)], f_s), (r1, z1_s), (r2, z2_s)):
            sent(ref, sem)

    entry_sent()


def body(tokens, gate_weight, up_weight, down_weight):
    V = pltpu.VMEM
    D = pltpu.SemaphoreType.DMA
    result = pl.pallas_call(
        kernel,
        out_shape=jax.ShapeDtypeStruct((XB, ROWS), BF),
        in_specs=[pl.BlockSpec(memory_space=pl.ANY)] * 4,
        out_specs=pl.BlockSpec(memory_space=V),
        scratch_shapes=[
            V((2 * NJ, K, 2 * FB), BF),
            V((FF, K), BF),
            V((NI, 4, 4, XB, R), BF),
            V((2, R, K), BF),
            V((S, R, 2 * FB), BF),
            V((S, R, 2 * FB), BF),
            V((S, R, 2 * FB), BF),
            V((R, 2 * FB), F32),
            V((S, 6, Q, FB), BF),
            V((NI, R, FF), BF),
            V((NI, 4, 4, XB, R), BF),
            V((NI, 2, 3, 4, HB, R), BF),
            V((NI, 2, 3, HB, R), BF),
            D((2 * NJ,)), D(()), D(()),
            D(()), D((NI,)), D(()), D((NI,)),
            D(()), D((S,)), D(()), D((S,)), D((S,)), D(()), D((S,)), D((S,)), D(()), D((NI,)),
            D(()), D((NI,)), D(()), D((NI,)),
        ],
        compiler_params=pltpu.CompilerParams(
            collective_id=0, has_side_effects=True, vmem_limit_bytes=60 * 2**20),
    )(tokens.T, gate_weight, up_weight, down_weight)
    return result.T


def solution(mesh):
    placed = (P(None, ("gx", "yz")), P("gx", "yz"), P("gx", "yz"), P("yz", "gx"))
    return jax.shard_map(
        body, mesh=mesh, in_specs=placed, out_specs=P(None, ("gx", "yz")), check_vma=False
    )
```

time: 265 us -> 85.4 us (0.32)
  waiting for transfers between devices: 217 us -> 0 us
  Pallas kernels: 0 us -> 82.9 us
  matrix products: 30.8 us -> 0 us
  between operations: 13.1 us -> 0.01 us
    reduce_scatter x3 -> x0, waiting for transfers between devices: 137 us -> none  [the longest x1 75.2 us: body(): lax.psum_scatter(terms.astype(jnp.bfloat16), 'yz', scatter_dimension=1, t...]
    pallas_call x0 -> x1, Pallas kernels: none -> 82.9 us  [body(): pl.pallas_call(kernel, out_shape=jax.ShapeDtypeStruct((XB, ROWS), BF), in...]
    all_gather x2 -> x0, waiting for transfers between devices: 78.8 us -> none  [the longest x1 50.5 us: body(): piece = lax.all_gather(tokens, 'yz', axis=1, tiled=True)]
    dot_general x3 -> x0, matrix products: 30.8 us -> none  [the longest x1 10.5 us: body(): up_part = jnp.dot(piece, up_weight, preferred_element_type=jnp.float32)]
  transfers between devices with their start and end apart: 5 -> 0, of which waited for: 5 -> 0; matrix products, arithmetic and copies ran while one was open for 4% -> 0% of each run, Pallas kernels for 0% -> 0%
where the time goes in v2:
time: 85.4 us; the launch traced here: 84.5 us
  Pallas kernels  82.9 us (97%)
  local copies, waits for them, and re-layouts  1.58 us (2%)
    pallas_call x1, Pallas kernels, body(): pl.pallas_call(kernel, out_shape=jax.ShapeDtypeStruct((XB, ROWS), BF), in...  82.9 us

profile of v2, /device:TPU:0, one launch (start us, length us, event | category | flops | bytes accessed | tf_op | source)
XLA Modules:
  0.0 84.5 jit_solution(4101712625359369388)
XLA Ops:
  0.0 82.9 %shard_map.46 = bf16[96,768]{1,0:T(8,128)(2,1)} custom-call(bf16[96,768]{1,0:T(8,128)(2,1)} %bitcast.3, bf16[1536,2304]{1,0:T(8,128)(2,1)} %wg_hbm.1, bf16[1536,2304]{1,0:T(8,128)(2,1)} %wu_hbm.1, bf16[2304,1536]{1,0:T(8,128)(2,1)} %wd_hbm.1), custom_call_target="tpu_custom_call" | custom-call | tf_op jit(solution)/shard_map/pallas_call | solution.py:346
  82.9 1.6 %copy.6 = bf16[768,96]{0,1:T(8,128)(2,1)} copy(bf16[768,96]{0,1:T(8,128)(2,1)} %bitcast.2) | data formatting | bytes 294912

commit v3 on v2

--- a/solution.py
+++ b/solution.py
@@ -21,14 +21,20 @@
 XB = 96
 HB = XB // 2
 
-LC, LD, LE, LF, LG, LZ, LO = 3, 5, 7, 9, 10, 12, 14
-DIRECT = S - 1
+LAGS = 2, 4, 6, 8, 9, 13, 16
+LC, LD, LE, LF, LG, LZ, LO = LAGS
+LS = 2
+NT = 2
+DIRECT = S - 3
+
+
+OTHERS = sorted(((kz, kx) for kz in range(4) for kx in range(4) if kz or kx), key=lambda k: -sum(min(v, 4 - v) for v in k))
 
 
 def kernel(tok_hbm, wg_hbm, wu_hbm, wd_hbm, out,
            wgu, wd, tok, tokr, sibs, sibr, par, own, yr, hid, terms, r1, r2,
            w_sem, wd_sem, tl_sem, t1_s, t1_r, t2_s, t2_r,
-           d_s, d_r, y_s, c_r, e_r, h_s, h_r, hf_r, f_s, f_r, z1_s, z1_r, z2_s, z2_r):
+           d_s, d_r, y_s, c_r, e_r, h_s, h_r, hf_r, f_s, f_r, z1_s, z1_r, z2_s, z2_r, l_s):
     g = lax.axis_index("gx")
     s_ = lax.axis_index("yz")
     y, c = g // 2, g % 2
@@ -46,6 +52,9 @@
     def at_x(k):
         return (g, z * 4 + m4(x + k))
 
+    def at_zx(kz, kx):
+        return (g, m4(z + kz) * 4 + m4(x + kx))
+
     def rc(src, dst, ss, rs, dev):
         return pltpu.make_async_remote_copy(
             src_ref=src, dst_ref=dst, send_sem=ss, recv_sem=rs,
@@ -66,7 +75,7 @@
     A, B = pl.ds(0, HB), pl.ds(HB, HB)
 
     barrier = pltpu.get_barrier_semaphore()
-    partners = [sib_dev, yp, ym, yo] + [f(k) for k in (1, 2, 3) for f in (at_z, at_x)]
+    partners = [sib_dev, yp, ym, yo] + [at_zx(kz, kx) for kz, kx in OTHERS]
     for dev in partners:
         pl.semaphore_signal(barrier, inc=1, device_id=dev, device_id_type=MESH)
 
@@ -100,14 +109,17 @@
         wd_copy.start()
 
     def t1_copy(i, h, k):
-        cols = pl.ds(pl.multiple_of(i * R, R), R)
         half = A if h == 0 else B
-        return rc(tok_hbm.at[half, cols], tok.at[i, z, x, half], t1_s, t1_r.at[i],
+        return rc(tok.at[i, z, x, half], tok.at[i, z, x, half], t1_s, t1_r.at[i],
                   at_x(k) if h == 0 else at_z(k))
 
     def t2_copy(i, h, k):
         blk = tok.at[i, z, :, A] if h == 0 else tok.at[i, :, x, B]
         return rc(blk, blk, t2_s, t2_r.at[i], at_z(k) if h == 0 else at_x(k))
+
+    def t0_start():
+        for kz, kx in OTHERS:
+            rc(tok.at[0, z, x], tok.at[0, z, x], l_s, t2_r.at[0], at_zx(kz, kx)).start()
 
     BOTH = [(h, k) for k in (2, 1, 3) for h in (0, 1)]
 
@@ -121,7 +133,14 @@
             t2_copy(i, h, k).start()
 
     def tok_ready(i):
-        arrived(r1.at[i], t2_r.at[i])
+        @pl.when(i == 0)
+        def _():
+            arrived(r2.at[pl.ds(0, 5)], t2_r.at[0])
+
+        @pl.when(i > 0)
+        def _():
+            arrived(r1.at[i], t2_r.at[i])
+
         tokr[i % 2] = tok[i].reshape(K, R).T
 
     def entry_barrier():
@@ -130,12 +149,12 @@
     def entry_own():
         pltpu.make_async_copy(tok.at[:, 0, 0], tok.at[:, 0, 0], tl_sem).wait()
 
+    entry_own()
     entry_barrier()
-    tok_first(0)
+    t0_start()
     weights_start()
-    entry_own()
-    tok_second(0)
     tok_first(1)
+    tok_second(1)
 
     def d_copy(s):
         return rc(sibs.at[s], sibr.at[s], d_s, d_r.at[s], sib_dev)
@@ -156,7 +175,9 @@
 
         @pl.when((j == 0) & (i + 1 < NI))
         def _():
-            tok_second(i + 1)
+            @pl.when(i > 0)
+            def _():
+                tok_second(i + 1)
 
             @pl.when(i + 2 < NI)
             def _():
@@ -291,16 +312,16 @@
             out[half, cols] = v.astype(BF)
 
     def step(u, _):
-        t = u - 1
+        t = u - LS
 
         @pl.when((t >= 0) & (t < S))
         def _():
             stage_own(t)
             stage_merge(t)
 
-        @pl.when(t + 1 < S)
-        def _():
-            stage_sib(t + 1)
+        @pl.when(t + LS < S)
+        def _():
+            stage_sib(t + LS)
 
         def lag(n, f):
             s = t - n
@@ -312,7 +333,7 @@
         def lag_i(n, f, most):
             s = t - n
 
-            @pl.when((s >= 0) & (s < most * NJ) & (lax.rem(s + S, NJ) == NJ - 1))
+            @pl.when((s >= 0) & (s < most * NJ) & (lax.rem(s + 2 * S, NJ) == NJ - 1))
             def _():
                 f(s // NJ)
 
@@ -320,20 +341,37 @@
         lag(LD, stage_d)
         lag(LE, stage_e)
         lag(LF, stage_f)
-        lag_i(LG, stage_g, NI - 1)
-        lag_i(LZ, stage_z, NI - 2)
-        lag_i(LO, stage_out, NI - 2)
+        lag_i(LG, stage_g, NI - 2)
+        lag_i(LZ, stage_z, NT)
+        lag_i(LO, stage_out, NT)
         return 0
 
-    lax.fori_loop(0, S + LF + 1, step, 0)
-    stage_g(NI - 1)
-    stage_z(NI - 2)
-    stage_z(NI - 1)
-    stage_out(NI - 2)
-    stage_out(NI - 1)
+    lax.fori_loop(0, S + LD + LS, step, 0)
+    for s in range(S + LD - LF, S + LD - LE):
+        stage_f(s)
+    for s in range(S + LD - LE, S - 1):
+        stage_e(s)
+        stage_f(s)
+
+    def last(n, _):
+        i = NI - 2 + n
+
+        @pl.when(n == 1)
+        def _():
+            stage_e(S - 1)
+            stage_f(S - 1)
+
+        stage_g(i)
+        return 0
+
+    lax.fori_loop(0, 2, last, 0)
+    for i in range(NT, NI):
+        stage_z(i)
+    for i in range(NT, NI):
+        stage_out(i)
 
     def entry_sent():
-        for ref, sem in ((r2, t1_s), (r1, t2_s), (sibs, d_s), (yr, y_s), (yr.at[:, pl.ds(0, 3)], h_s),
+        for ref, sem in ((r2.at[pl.ds(1, NI - 1)], t1_s), (r1.at[pl.ds(1, NI - 1)], t2_s), (r2.at[pl.ds(0, 5)], l_s), (sibs, d_s), (yr, y_s), (yr.at[:, pl.ds(0, 3)], h_s),
                          (hid.at[:, :, pl.ds(0, FF // 2)], f_s), (r1, z1_s), (r2, z2_s)):
             sent(ref, sem)
 
@@ -365,7 +403,7 @@
             D((2 * NJ,)), D(()), D(()),
             D(()), D((NI,)), D(()), D((NI,)),
             D(()), D((S,)), D(()), D((S,)), D((S,)), D(()), D((S,)), D((S,)), D(()), D((NI,)),
-            D(()), D((NI,)), D(()), D((NI,)),
+            D(()), D((NI,)), D(()), D((NI,)), D(()),
         ],
         compiler_params=pltpu.CompilerParams(
             collective_id=0, has_side_effects=True, vmem_limit_bytes=60 * 2**20),

time: 85.4 us -> 80.5 us (0.943)
  Pallas kernels: 82.9 us -> 78.7 us
    pallas_call x1, Pallas kernels: 82.9 us -> 78.7 us  [body(): pl.pallas_call(kernel, out_shape=jax.ShapeDtypeStruct((XB, ROWS), BF), in...]
where the time goes in v3:
time: 80.5 us; the launch traced here: 80.3 us
  Pallas kernels  78.7 us (98%)
  local copies, waits for them, and re-layouts  1.58 us (2%)
    pallas_call x1, Pallas kernels, body(): pl.pallas_call(kernel, out_shape=jax.ShapeDtypeStruct((XB, ROWS), BF), in...  78.7 us

profile of v3, /device:TPU:0, one launch (start us, length us, event | category | flops | bytes accessed | tf_op | source)
XLA Modules:
  0.0 80.3 jit_solution(17802104114823904938)
XLA Ops:
  0.0 78.7 %shard_map.46 = bf16[96,768]{1,0:T(8,128)(2,1)} custom-call(bf16[96,768]{1,0:T(8,128)(2,1)} %bitcast.3, bf16[1536,2304]{1,0:T(8,128)(2,1)} %wg_hbm.1, bf16[1536,2304]{1,0:T(8,128)(2,1)} %wu_hbm.1, bf16[2304,1536]{1,0:T(8,128)(2,1)} %wd_hbm.1), custom_call_target="tpu_custom_call" | custom-call | tf_op jit(solution)/shard_map/pallas_call | solution.py:384
  78.7 1.6 %copy.6 = bf16[768,96]{0,1:T(8,128)(2,1)} copy(bf16[768,96]{0,1:T(8,128)(2,1)} %bitcast.2) | data formatting | bytes 294912

commit v4 on v3

--- a/solution.py
+++ b/solution.py
@@ -24,6 +24,7 @@
 LAGS = 2, 4, 6, 8, 9, 13, 16
 LC, LD, LE, LF, LG, LZ, LO = LAGS
 LS = 2
+NS = 9
 NT = 2
 DIRECT = S - 3
 
@@ -101,12 +102,13 @@
 
     wd_copy = pltpu.make_async_copy(wd_hbm, wd, wd_sem)
 
-    def weights_start():
-        for j in range(NJ):
+    def weights_start(some):
+        for j in some:
             for b in (b_sib(j), b_own(j)):
                 for cp in w_copies(b):
                     cp.start()
-        wd_copy.start()
+        if NJ - 1 in some:
+            wd_copy.start()
 
     def t1_copy(i, h, k):
         half = A if h == 0 else B
@@ -151,13 +153,14 @@
 
     entry_own()
     entry_barrier()
+    weights_start(range(1))
     t0_start()
-    weights_start()
     tok_first(1)
+    weights_start(range(1, NJ))
     tok_second(1)
 
     def d_copy(s):
-        return rc(sibs.at[s], sibr.at[s], d_s, d_r.at[s], sib_dev)
+        return rc(sibs.at[s], sibr.at[s], d_s, d_r.at[s % NS], sib_dev)
 
     def stage_sib(s):
         i, j = s // NJ, s % NJ
@@ -192,26 +195,22 @@
 
         own[...] = jnp.dot(tokr[i % 2], wgu[b_own(j)], preferred_element_type=F32)
 
-    G, U = pl.ds(0, FB), pl.ds(FB, FB)
-
     def y_copy(s, n):
-        q, cols, dev = ((2, G, yp), (2, U, ym), (1, U, yp), (3, G, ym), (1, G, yp), (3, U, ym))[n]
-        return rc(par.at[s, rows(m4(y + q), Q), cols], yr.at[s, n], y_s, (c_r if n < 2 else e_r).at[s], dev)
+        ahead = 1 + 2 * (s % 2)
+        q, to = ((2, ahead), (4 - ahead, 4 - ahead), (ahead, ahead))[n]
+        return rc(par.at[s, rows(m4(y + q), Q)], yr.at[s, n], y_s, (e_r if n else c_r).at[s % NS], (m4(y + to) * 2 + c, s_))
 
     def stage_merge(s):
-        arrived(sibr.at[s], d_r.at[s])
+        arrived(sibr.at[s], d_r.at[s % NS])
         par[s] = (own[...] + sibr[s].astype(F32)).astype(BF)
-        for n in range(4):
+        for n in range(2):
             y_copy(s, n).start()
 
     def stage_c(s):
-        arrived(yr.at[s, pl.ds(0, 2)], c_r.at[s])
-        rr = rows(m4(y + 1), Q)
-        par[s, rr, G] = (par[s, rr, G].astype(F32) + yr[s, 0].astype(F32)).astype(BF)
-        y_copy(s, 4).start()
-        rr = rows(m4(y + 3), Q)
-        par[s, rr, U] = (par[s, rr, U].astype(F32) + yr[s, 1].astype(F32)).astype(BF)
-        y_copy(s, 5).start()
+        arrived(yr.at[s, 0], c_r.at[s % NS])
+        rr = rows(m4(y + 1 + 2 * (s % 2)), Q)
+        par[s, rr, :] = (par[s, rr, :].astype(F32) + yr[s, 0].astype(F32)).astype(BF)
+        y_copy(s, 2).start()
 
     def h_block(s, k):
         i, j = s // NJ, s % NJ
@@ -219,7 +218,7 @@
 
     def h_copy(s, d):
         blk = h_block(s, 0)
-        return rc(blk, blk, h_s, h_r.at[s], yp if d == 0 else ym)
+        return rc(blk, blk, h_s, h_r.at[s % NS], yp if d == 0 else ym)
 
     def hf_copy(s, d):
         blk = h_block(s, 3 if d == 0 else 1)
@@ -231,10 +230,10 @@
 
     def stage_d(s):
         i, j = s // NJ, s % NJ
-        arrived(yr.at[s, pl.ds(2, 4)], e_r.at[s])
+        arrived(yr.at[s, pl.ds(1, 2)], e_r.at[s % NS])
         rr = rows(y, Q)
-        gate = par[s, rr, G].astype(F32) + (yr[s, 3].astype(F32) + yr[s, 4].astype(F32))
-        up = par[s, rr, U].astype(F32) + (yr[s, 2].astype(F32) + yr[s, 5].astype(F32))
+        both = par[s, rr, :].astype(F32) + (yr[s, 1].astype(F32) + yr[s, 2].astype(F32))
+        gate, up = both[:, :FB], both[:, FB:]
         hid[i, rr, lanes(b_own(j), FB)] = (gate / (1.0 + jnp.exp(-gate)) * up).astype(BF)
         @pl.when(s >= DIRECT)
         def _():
@@ -244,13 +243,13 @@
             h_copy(s, d).start()
 
     def stage_e(s):
-        arrived(yr.at[s, pl.ds(0, 2)], h_r.at[s])
+        arrived(yr.at[s, 0], h_r.at[s % NS])
+
+        @pl.when((s < DIRECT) & (s % 2 == 1))
+        def _():
+            hf_copy(s, 0).start()
 
         @pl.when((s < DIRECT) & (s % 2 == 0))
-        def _():
-            hf_copy(s, 0).start()
-
-        @pl.when((s < DIRECT) & (s % 2 == 1))
         def _():
             hf_copy(s, 1).start()
 
@@ -260,7 +259,7 @@
         return rc(blk, blk, f_s, f_r.at[i], sib_dev)
 
     def stage_f(s):
-        arrived(yr.at[s, 0], hf_r.at[s])
+        arrived(yr.at[s, 0, :, pl.ds(0, FB)], hf_r.at[s])
         f_copy(s, c).start()
 
     def z1_copy(i, h, k):
@@ -342,7 +341,7 @@
         lag(LE, stage_e)
         lag(LF, stage_f)
         lag_i(LG, stage_g, NI - 2)
-        lag_i(LZ, stage_z, NT)
+        lag_i(LZ, stage_z, NT + 1)
         lag_i(LO, stage_out, NT)
         return 0
 
@@ -365,13 +364,13 @@
         return 0
 
     lax.fori_loop(0, 2, last, 0)
-    for i in range(NT, NI):
+    for i in range(NT + 1, NI):
         stage_z(i)
     for i in range(NT, NI):
         stage_out(i)
 
     def entry_sent():
-        for ref, sem in ((r2.at[pl.ds(1, NI - 1)], t1_s), (r1.at[pl.ds(1, NI - 1)], t2_s), (r2.at[pl.ds(0, 5)], l_s), (sibs, d_s), (yr, y_s), (yr.at[:, pl.ds(0, 3)], h_s),
+        for ref, sem in ((r2.at[pl.ds(1, NI - 1)], t1_s), (r1.at[pl.ds(1, NI - 1)], t2_s), (r2.at[pl.ds(0, 5)], l_s), (sibs, d_s), (yr, y_s), (yr.at[:, :, :, pl.ds(0, FB)], h_s),
                          (hid.at[:, :, pl.ds(0, FF // 2)], f_s), (r1, z1_s), (r2, z2_s)):
             sent(ref, sem)
 
@@ -395,14 +394,14 @@
             V((S, R, 2 * FB), BF),
             V((S, R, 2 * FB), BF),
             V((R, 2 * FB), F32),
-            V((S, 6, Q, FB), BF),
+            V((S, 3, Q, 2 * FB), BF),
             V((NI, R, FF), BF),
             V((NI, 4, 4, XB, R), BF),
             V((NI, 2, 3, 4, HB, R), BF),
             V((NI, 2, 3, HB, R), BF),
             D((2 * NJ,)), D(()), D(()),
             D(()), D((NI,)), D(()), D((NI,)),
-            D(()), D((S,)), D(()), D((S,)), D((S,)), D(()), D((S,)), D((S,)), D(()), D((NI,)),
+            D(()), D((NS,)), D(()), D((NS,)), D((NS,)), D(()), D((NS,)), D((S,)), D(()), D((NI,)),
             D(()), D((NI,)), D(()), D((NI,)), D(()),
         ],
         compiler_params=pltpu.CompilerParams(

time: 80.5 us -> 80 us (level)
  Pallas kernels: 78.7 us -> 77.8 us
    pallas_call x1, Pallas kernels: 78.7 us -> 77.8 us  [body(): pl.pallas_call(kernel, out_shape=jax.ShapeDtypeStruct((XB, ROWS), BF), in...]
where the time goes in v4:
time: 80 us; the launch traced here: 79.3 us
  Pallas kernels  77.8 us (97%)
  local copies, waits for them, and re-layouts  1.58 us (2%)
    pallas_call x1, Pallas kernels, body(): pl.pallas_call(kernel, out_shape=jax.ShapeDtypeStruct((XB, ROWS), BF), in...  77.8 us

profile of v4, /device:TPU:0, one launch (start us, length us, event | category | flops | bytes accessed | tf_op | source)
XLA Modules:
  0.0 79.3 jit_solution(12808754471409496196)
XLA Ops:
  0.0 77.8 %shard_map.46 = bf16[96,768]{1,0:T(8,128)(2,1)} custom-call(bf16[96,768]{1,0:T(8,128)(2,1)} %bitcast.3, bf16[1536,2304]{1,0:T(8,128)(2,1)} %wg_hbm.1, bf16[1536,2304]{1,0:T(8,128)(2,1)} %wu_hbm.1, bf16[2304,1536]{1,0:T(8,128)(2,1)} %wd_hbm.1), custom_call_target="tpu_custom_call" | custom-call | tf_op jit(solution)/shard_map/pallas_call | solution.py:383
  77.8 1.6 %copy.6 = bf16[768,96]{0,1:T(8,128)(2,1)} copy(bf16[768,96]{0,1:T(8,128)(2,1)} %bitcast.2) | data formatting | bytes 294912

commit v5 on v4

--- a/solution.py
+++ b/solution.py
@@ -33,7 +33,7 @@
 
 
 def kernel(tok_hbm, wg_hbm, wu_hbm, wd_hbm, out,
-           wgu, wd, tok, tokr, sibs, sibr, par, own, yr, hid, terms, r1, r2,
+           wgu, wd, tok, tokr, sibs, sibr, par, own, acc, yr, hid, terms, r1, r2,
            w_sem, wd_sem, tl_sem, t1_s, t1_r, t2_s, t2_r,
            d_s, d_r, y_s, c_r, e_r, h_s, h_r, hf_r, f_s, f_r, z1_s, z1_r, z2_s, z2_r, l_s):
     g = lax.axis_index("gx")
@@ -256,7 +256,7 @@
     def f_copy(s, half):
         i, j = s // NJ, s % NJ
         blk = hid.at[i, :, lanes(half * NJ + j, FB)]
-        return rc(blk, blk, f_s, f_r.at[i], sib_dev)
+        return rc(blk, blk, f_s, f_r.at[i + s // (S - 1)], sib_dev)
 
     def stage_f(s):
         arrived(yr.at[s, 0, :, pl.ds(0, FB)], hf_r.at[s])
@@ -287,6 +287,29 @@
             p = mine if n else 1 - mine
             res = jnp.dot(hid[i], wd[:, lanes(p, K // 2)], preferred_element_type=F32).astype(BF)
             terms[i, pl.ds(2 * p, 2)] = res.T.reshape(2, 4, XB, R)
+        for h, k in BOTH:
+            z1_copy(i, h, k).start()
+
+    def part(js, cols):
+        i, total = NI - 1, 0.0
+        for half in range(2):
+            k = pl.ds((half * NJ + js[0]) * FB, len(js) * FB)
+            total = total + jnp.dot(hid[i, :, k], wd[k, cols], preferred_element_type=F32)
+        return total
+
+    def stage_part():
+        arrived(hid.at[NI - 1, :, pl.ds(0, (NJ - 1) * FB)], f_r.at[NI - 1])
+        for n in range(2):
+            cols = pl.ds(n * (K // 2), K // 2)
+            acc[:, cols] = part(range(NJ - 1), cols)
+
+    def stage_rest():
+        i = NI - 1
+        arrived(hid.at[i, :, pl.ds(0, FB)], f_r.at[NI])
+        for n in range(2):
+            cols = pl.ds(n * (K // 2), K // 2)
+            res = (acc[:, cols] + part([NJ - 1], cols)).astype(BF)
+            terms[i, pl.ds(2 * n, 2)] = res.T.reshape(2, 4, XB, R)
         for h, k in BOTH:
             z1_copy(i, h, k).start()
 
@@ -352,18 +375,11 @@
         stage_e(s)
         stage_f(s)
 
-    def last(n, _):
-        i = NI - 2 + n
-
-        @pl.when(n == 1)
-        def _():
-            stage_e(S - 1)
-            stage_f(S - 1)
-
-        stage_g(i)
-        return 0
-
-    lax.fori_loop(0, 2, last, 0)
+    stage_g(NI - 2)
+    stage_part()
+    stage_e(S - 1)
+    stage_f(S - 1)
+    stage_rest()
     for i in range(NT + 1, NI):
         stage_z(i)
     for i in range(NT, NI):
@@ -394,6 +410,7 @@
             V((S, R, 2 * FB), BF),
             V((S, R, 2 * FB), BF),
             V((R, 2 * FB), F32),
+            V((R, K), F32),
             V((S, 3, Q, 2 * FB), BF),
             V((NI, R, FF), BF),
             V((NI, 4, 4, XB, R), BF),
@@ -401,7 +418,7 @@
             V((NI, 2, 3, HB, R), BF),
             D((2 * NJ,)), D(()), D(()),
             D(()), D((NI,)), D(()), D((NI,)),
-            D(()), D((NS,)), D(()), D((NS,)), D((NS,)), D(()), D((NS,)), D((S,)), D(()), D((NI,)),
+            D(()), D((NS,)), D(()), D((NS,)), D((NS,)), D(()), D((NS,)), D((S,)), D(()), D((NI + 1,)),
             D(()), D((NI,)), D(()), D((NI,)), D(()),
         ],
         compiler_params=pltpu.CompilerParams(

time: 80 us -> 79.5 us (level)
  no operation moved by 1% of the time
where the time goes in v5:
time: 79.5 us; the launch traced here: 79.3 us
  Pallas kernels  77.8 us (98%)
  local copies, waits for them, and re-layouts  1.58 us (2%)
    pallas_call x1, Pallas kernels, body(): pl.pallas_call(kernel, out_shape=jax.ShapeDtypeStruct((XB, ROWS), BF), in...  77.8 us

profile of v5, /device:TPU:0, one launch (start us, length us, event | category | flops | bytes accessed | tf_op | source)
XLA Modules:
  0.0 79.3 jit_solution(17818838009894294332)
XLA Ops:
  0.0 77.8 %shard_map.46 = bf16[96,768]{1,0:T(8,128)(2,1)} custom-call(bf16[96,768]{1,0:T(8,128)(2,1)} %bitcast.3, bf16[1536,2304]{1,0:T(8,128)(2,1)} %wg_hbm.1, bf16[1536,2304]{1,0:T(8,128)(2,1)} %wu_hbm.1, bf16[2304,1536]{1,0:T(8,128)(2,1)} %wd_hbm.1), custom_call_target="tpu_custom_call" | custom-call | tf_op jit(solution)/shard_map/pallas_call | solution.py:399
  77.8 1.6 %copy.6 = bf16[768,96]{0,1:T(8,128)(2,1)} copy(bf16[768,96]{0,1:T(8,128)(2,1)} %bitcast.2) | data formatting | bytes 294912
